TPU v7x, 512 devices: a whole 4x4x16 slice. The times are simulated.
512 devices in a mesh: row: 16 (over x, z_hi, core), col: 8 (over z_lo), depth: 4 (over y).
Axes of the slice: x: 4, y: 4, z: 16 (z_hi: 2, z_lo: 8; z = z_hi * 8 + z_lo), core: 2. Of those that a mesh axis runs over, the one named last changes fastest.
Arguments:
- a_blocks: float32 [16, 8, 4, 4, 128, 128], P('row', 'col', 'depth'), may hold values from -0.5 to 0.5
- b_blocks: float32 [16, 8, 4, 4, 128, 128], P('row', 'col', 'depth'), may hold values from -1 to 1
- triples: int32 [16, 8, 4, 16, 16, 3], P('row', 'col', 'depth'), may hold values from 0 to 31, as said below
- live: int32 [16, 8, 4, 16], P('row', 'col', 'depth'), may hold values from 1 to 16, as said below
- c_order: int32 [16, 8, 16], P('row', 'col'), may hold values from 0 to 15, as said below
Outputs:
- c_blocks: float32 [16, 8, 4, 4, 128, 128], P('row', 'col', 'depth')
Inputs may be any that keep to these rules, and one draw needn't show every extreme that they name: `triples`: in each triple the first entry is below 32, the second below 4, the third below 16. `live`: loads differ strongly between devices. For each grid position (r, c), c_order[r, c] names each of its 16 product slots exactly once; different grid positions have independent orders.
All inputs are finite; a program needn't handle non-finite values.
Results may differ from a plain program's by a relative error of at most 0.0003.
Values sent between devices are 32-bit elements; how exact they have to be, the bound alone decides.
A program may use at most 64 MiB of HBM per device.

v0:
```python
import jax
import jax.numpy as jnp
from jax import lax
from jax.sharding import PartitionSpec as P


def block_products(a_panel, b_shard, triple_rows, live_count, running):
    width = triple_rows.shape[0]
    left_blocks = jnp.take(a_panel, triple_rows[:, 0], axis=0)
    right_blocks = jnp.take(b_shard, triple_rows[:, 1], axis=0)
    products = jnp.einsum(
        "tik,tkj->tij", left_blocks, right_blocks, precision=lax.Precision.HIGHEST
    )
    active_mask = (jnp.arange(width, dtype=jnp.int32) < live_count).astype(jnp.float32)
    slot_ids = jnp.arange(running.shape[0], dtype=jnp.int32)
    placing = (triple_rows[:, 2][None, :] == slot_ids[:, None]).astype(jnp.float32) * active_mask[
        None, :
    ]
    return running + jnp.einsum("ct,tij->cij", placing, products, precision=lax.Precision.HIGHEST)


def on_device(a_blocks, b_blocks, triples, live, c_order):
    block_side = a_blocks.shape[-1]
    gathered = lax.all_gather(a_blocks, "col", axis=1, tiled=True)
    a_panel = gathered.reshape(-1, block_side, block_side)
    triple_table = triples[0, 0, 0]
    live_table = live[0, 0, 0]
    slot_order = c_order[0, 0]
    slot_total = slot_order.shape[0]
    initial = jnp.zeros((slot_total, block_side, block_side), jnp.float32)
    pieces = lax.all_gather(b_blocks, "row", axis=0, tiled=True)
    shards = pieces.reshape(-1, pieces.shape[3], block_side, block_side)

    def one_step(offset, running):
        b_shard = lax.dynamic_index_in_dim(shards, offset, 0, keepdims=False)
        triple_rows = lax.dynamic_index_in_dim(triple_table, offset, 0, keepdims=False)
        live_count = lax.dynamic_index_in_dim(live_table, offset, 0, keepdims=False)
        return block_products(a_panel, b_shard, triple_rows, live_count, running)

    partial_sum = lax.fori_loop(0, shards.shape[0], one_step, initial)
    share_count = slot_total // lax.axis_size("depth")
    summed_all = lax.psum(partial_sum, "depth")
    owned_slots = lax.dynamic_slice_in_dim(
        slot_order, lax.axis_index("depth") * share_count, share_count, 0
    )
    owned_blocks = jnp.take(summed_all, owned_slots, axis=0)
    return owned_blocks.reshape(1, 1, 1, share_count, block_side, block_side)


def solution(mesh):
    placed = (
        P("row", "col", "depth", None, None, None),
        P("row", "col", "depth", None, None, None),
        P("row", "col", "depth", None, None, None),
        P("row", "col", "depth", None),
        P("row", "col", None),
    )
    return jax.shard_map(
        on_device,
        mesh=mesh,
        in_specs=placed,
        out_specs=P("row", "col", "depth", None, None, None),
        check_vma=False,
    )
```

profile of v0, /device:TPU:1, one launch (start us, length us, event | category | flops | bytes accessed | tf_op | source)
XLA Modules:
  0.0 431.1 jit_solution(8318842052814927611)
XLA Ops:
  8.8 71.8 %all-gather.3.cloned.1.call-done = f32[1,8,1,4,128,128]{5,4,3,2,0,1:T(8,128)} async-done(((f32[1,1,1,4,128,128]{5,4,3,2,0,1:T(8,128)}), f32[1,8,1,4,128,128]{5,4,3,2,0,1:T(8,128)}) %all-gather.3.cloned.1.call-update) | async-done | bytes 2097168 | tf_op jit(solution)/shard_map/all_gather | solution.py:24
  80.6 123.9 %all-gather.5.cloned.1.call-done = f32[16,1,1,4,128,128]{5,4,3,2,1,0:T(8,128)} async-done(((f32[1,1,1,4,128,128]{5,4,3,2,1,0:T(8,128)}), f32[16,1,1,4,128,128]{5,4,3,2,1,0:T(8,128)}) %all-gather.5.cloned.1.call-update) | async-done | bytes 4194320 | tf_op jit(solution)/shard_map/all_gather | solution.py:31
  204.5 162.5 %while.14 = (s32[]{:T(128)}, f32[16,128,128]{2,0,1:T(8,128)}, s32[16,16,3]{1,2,0:T(4,128)S(1)}, s32[16]{0:T(128)}, f32[32,128,128]{2,1,0:T(8,128)}, /*index=5*/f32[16,4,128,128]{3,2,1,0:T(8,128)}, s32[]{:T(128)}, s32[]{:T(128)}) while((s32[]{:T(128)}, f32[16,128,128]{2,0,1:T(8,128)}, s32[16,16,3]{1,2,0:T(4,128)S(1)}, s32[16]{0:T(128)}, ...), condition=%wide.region_1.2_spmd.clone, body=%wide.region_0.1_spmd.clone.sunk | while | flops 454036288 | bytes 11020059 | solution.py:40
  211.0 2.5 convolution_add_fusion.2
  220.0 3.7 convolution_add_fusion.2
  225.4 2.2 gather_fusion.1
  230.2 3.7 convolution_add_fusion.2
  235.6 2.2 gather_fusion.1
  240.5 3.7 convolution_add_fusion.2
  245.8 2.2 gather_fusion.1
  250.7 3.7 convolution_add_fusion.2
  260.9 3.7 convolution_add_fusion.2
  271.2 3.7 convolution_add_fusion.2
  281.4 3.7 convolution_add_fusion.2
  291.6 3.7 convolution_add_fusion.2
  301.8 3.7 convolution_add_fusion.2
  312.1 3.7 convolution_add_fusion.2
  322.3 3.7 convolution_add_fusion.2
  332.5 3.7 convolution_add_fusion.2
  342.8 3.7 convolution_add_fusion.2
  353.0 3.7 convolution_add_fusion.2
  363.2 3.7 convolution_add_fusion.2
  366.9 2.5 copy.14
  369.7 52.3 %all-reduce.2.cloned.1.call-done = f32[16,128,128]{2,1,0:T(8,128)} async-done(((f32[16,128,128]{2,1,0:T(8,128)}), f32[16,128,128]{2,1,0:T(8,128)}) %all-reduce.2.cloned.1.call-update) | async-done | bytes 1048592 | tf_op jit(solution)/shard_map/psum | solution.py:42
  (204 shorter events, 101.3 us)
Async XLA Ops:
  6.5 74.1 %all-gather.3.cloned.1.call-start = ((), (), s32[]{:S(2)}) async-start(), calls=%async_computation | async-start | bytes 2359296 | tf_op jit(solution)/shard_map/all_gather | solution.py:24
  7.3 197.2 %all-gather.5.cloned.1.call-start = ((), (), s32[]{:S(2)}) async-start(), calls=%async_computation.1 | async-start | bytes 4456448 | tf_op jit(solution)/shard_map/all_gather | solution.py:31
  8.0 414.0 %all-reduce.2.cloned.1.call-start = ((), (), s32[]{:S(2)}) async-start(), calls=%async_computation.2 | async-start | bytes 2097152 | tf_op jit(solution)/shard_map/psum | solution.py:42
  204.5 165.0 %copy-start.1 = (s32[1,1,16]{2,1,0:T(1,128)S(1)}, s32[1,1,16]{2,1,0:T(1,128)}, u32[]{:S(2)}) copy-start(s32[1,1,16]{2,1,0:T(1,128)} %param.11) | copy-start | bytes 196
  204.5 5.2 %copy-start = (s32[16]{0:T(128)S(1)}, s32[16]{0:T(128)}, u32[]{:S(2)}) copy-start(s32[16]{0:T(128)} %get-tuple-element.225) | copy-start | bytes 196 | tf_op jit(solution)/shard_map/while
  213.5 5.2 %copy-start = (s32[16]{0:T(128)S(1)}, s32[16]{0:T(128)}, u32[]{:S(2)}) copy-start(s32[16]{0:T(128)} %get-tuple-element.225) | copy-start | bytes 196 | tf_op jit(solution)/shard_map/while
  223.7 5.2 %copy-start = (s32[16]{0:T(128)S(1)}, s32[16]{0:T(128)}, u32[]{:S(2)}) copy-start(s32[16]{0:T(128)} %get-tuple-element.225) | copy-start | bytes 196 | tf_op jit(solution)/shard_map/while
  234.0 5.2 %copy-start = (s32[16]{0:T(128)S(1)}, s32[16]{0:T(128)}, u32[]{:S(2)}) copy-start(s32[16]{0:T(128)} %get-tuple-element.225) | copy-start | bytes 196 | tf_op jit(solution)/shard_map/while
  244.2 5.2 %copy-start = (s32[16]{0:T(128)S(1)}, s32[16]{0:T(128)}, u32[]{:S(2)}) copy-start(s32[16]{0:T(128)} %get-tuple-element.225) | copy-start | bytes 196 | tf_op jit(solution)/shard_map/while
  254.4 5.2 %copy-start = (s32[16]{0:T(128)S(1)}, s32[16]{0:T(128)}, u32[]{:S(2)}) copy-start(s32[16]{0:T(128)} %get-tuple-element.225) | copy-start | bytes 196 | tf_op jit(solution)/shard_map/while
  264.6 5.2 %copy-start = (s32[16]{0:T(128)S(1)}, s32[16]{0:T(128)}, u32[]{:S(2)}) copy-start(s32[16]{0:T(128)} %get-tuple-element.225) | copy-start | bytes 196 | tf_op jit(solution)/shard_map/while
  274.9 5.2 %copy-start = (s32[16]{0:T(128)S(1)}, s32[16]{0:T(128)}, u32[]{:S(2)}) copy-start(s32[16]{0:T(128)} %get-tuple-element.225) | copy-start | bytes 196 | tf_op jit(solution)/shard_map/while
  285.1 5.2 %copy-start = (s32[16]{0:T(128)S(1)}, s32[16]{0:T(128)}, u32[]{:S(2)}) copy-start(s32[16]{0:T(128)} %get-tuple-element.225) | copy-start | bytes 196 | tf_op jit(solution)/shard_map/while
  295.3 5.2 %copy-start = (s32[16]{0:T(128)S(1)}, s32[16]{0:T(128)}, u32[]{:S(2)}) copy-start(s32[16]{0:T(128)} %get-tuple-element.225) | copy-start | bytes 196 | tf_op jit(solution)/shard_map/while
  305.6 5.2 %copy-start = (s32[16]{0:T(128)S(1)}, s32[16]{0:T(128)}, u32[]{:S(2)}) copy-start(s32[16]{0:T(128)} %get-tuple-element.225) | copy-start | bytes 196 | tf_op jit(solution)/shard_map/while
  315.8 5.2 %copy-start = (s32[16]{0:T(128)S(1)}, s32[16]{0:T(128)}, u32[]{:S(2)}) copy-start(s32[16]{0:T(128)} %get-tuple-element.225) | copy-start | bytes 196 | tf_op jit(solution)/shard_map/while
  326.0 5.2 %copy-start = (s32[16]{0:T(128)S(1)}, s32[16]{0:T(128)}, u32[]{:S(2)}) copy-start(s32[16]{0:T(128)} %get-tuple-element.225) | copy-start | bytes 196 | tf_op jit(solution)/shard_map/while
  336.2 5.2 %copy-start = (s32[16]{0:T(128)S(1)}, s32[16]{0:T(128)}, u32[]{:S(2)}) copy-start(s32[16]{0:T(128)} %get-tuple-element.225) | copy-start | bytes 196 | tf_op jit(solution)/shard_map/while
  346.5 5.2 %copy-start = (s32[16]{0:T(128)S(1)}, s32[16]{0:T(128)}, u32[]{:S(2)}) copy-start(s32[16]{0:T(128)} %get-tuple-element.225) | copy-start | bytes 196 | tf_op jit(solution)/shard_map/while
  356.7 5.2 %copy-start = (s32[16]{0:T(128)S(1)}, s32[16]{0:T(128)}, u32[]{:S(2)}) copy-start(s32[16]{0:T(128)} %get-tuple-element.225) | copy-start | bytes 196 | tf_op jit(solution)/shard_map/while
Sparse Core Ops, SparseCore 0:
  9.4 71.1 all-gather.2
  83.9 120.5 all-gather.4
  369.6 52.3 all-reduce.1
where the time goes:
time: 433 us; the launch traced here: 431 us
  waiting for transfers between devices  249 us (58%)
  matrix products  78.5 us (18%)
  local copies, waits for them, and re-layouts  76.6 us (18%)
  between operations  13.1 us (3%)
  other arithmetic  12.1 us (3%)
    all_gather x1, waiting for transfers between devices, on_device(): pieces = lax.all_gather(b_blocks, 'row', axis=0, tiled=True)  124 us
    all_gather x1, waiting for transfers between devices, on_device(): gathered = lax.all_gather(a_blocks, 'col', axis=1, tiled=True)  71.8 us
    dot_general x16, matrix products, block_products(): jnp.einsum('ct,tij->cij', placing, products, precision=lax.Precision.HIGH...  58.2 us
    psum x1, waiting for transfers between devices, on_device(): summed_all = lax.psum(partial_sum, 'depth')  52.3 us
    gather x16, local copies, waits for them, and re-layouts, block_products(): left_blocks = jnp.take(a_panel, triple_rows[:, 0], axis=0)  35.3 us
    dot_general x16, matrix products, block_products(): jnp.einsum('tik,tkj->tij', left_blocks, right_blocks, precision=lax.Preci...  20.3 us
    squeeze x16, local copies, waits for them, and re-layouts, one_step(): b_shard = lax.dynamic_index_in_dim(shards, offset, 0, keepdims=False)  15.7 us
    convert_element_type x16, other arithmetic, block_products(): (jnp.arange(width, dtype=jnp.int32) < live_count).astype(jnp.float32)  10.8 us
  transfers between devices with their start and end apart: 3, of which 3 were waited for; matrix products, arithmetic and copies ran while one was open for 0% of the time, Pallas kernels for 0%

commit v1 on v0

v1 whole, which is shorter than its diff:
```python
import functools

import jax
import jax.numpy as jnp
from jax import lax
from jax.experimental import pallas as pl
from jax.experimental.pallas import tpu as pltpu
from jax.sharding import PartitionSpec as P

MESH = pl.DeviceIdType.MESH
NX, NY, NZ, NC = 4, 4, 16, 8
STEPS, TCAP, SLOTS, OWN = 16, 16, 16, 4
HA, HB = 2, 4
B_START = (2, 4)


def split_pair(block):
    high = block.astype(jnp.bfloat16)
    low = (block - high.astype(jnp.float32)).astype(jnp.bfloat16)
    return jnp.concatenate([high, low], axis=-1)


def kernel(
    a_ref, b_ref, trip, live, order, out,
    abuf, bbuf, ahl, bhl, cum, sbuf, rbuf, prev, last,
    ss_a, rs_a, ss_x0, rs_x0, ss_k0, rs_k0, ss_z, rs_z, ss_x1, rs_x1, ss_k1, rs_k1, ss_c, rs_c,
):
    row, c, y = lax.axis_index("row"), lax.axis_index("col"), lax.axis_index("depth")
    x, zh, k = row // 4, (row // 2) % 2, row % 2

    def dev(dx=0, dz=0, dk=0, dc=0, dy=0):
        r = ((x + dx + NX) % NX) * 4 + ((zh + dz) % 2) * 2 + (k + dk) % 2
        return (r, c + dc, (y + dy + NY) % NY)

    def copy(src, dst, ss, rs, to):
        return pltpu.make_async_remote_copy(
            src_ref=src, dst_ref=dst, send_sem=ss, recv_sem=rs, device_id=to, device_id_type=MESH
        )

    barrier = pltpu.get_barrier_semaphore()
    partners = [dev(dx=1), dev(dx=2), dev(dx=3), dev(dz=1), dev(dk=1), dev(dy=1), dev(dy=2), dev(dy=3)]
    for p in partners:
        pl.semaphore_signal(barrier, inc=1, device_id=p, device_id_type=MESH)

    @pl.when(c > 0)
    def _():
        pl.semaphore_signal(barrier, inc=1, device_id=dev(dc=-1), device_id_type=MESH)

    @pl.when(c < NC - 1)
    def _():
        pl.semaphore_signal(barrier, inc=1, device_id=dev(dc=1), device_id_type=MESH)

    ends = (c > 0).astype(jnp.int32) + (c < NC - 1).astype(jnp.int32)
    pl.semaphore_wait(barrier, len(partners) + ends)

    wa = 4 // HA

    def a_copy(direction, t, h):
        j = c - t * direction
        part = pl.ds(h * wa, wa)
        src = a_ref.at[part] if t == 0 else abuf.at[j, part]
        return copy(
            src, abuf.at[j, part], ss_a.at[(1 - direction) // 2, t, h], rs_a.at[j, h], dev(dc=direction)
        )

    def a_arrived(j, h):
        part = pl.ds(h * wa, wa)
        copy(abuf.at[j, part], abuf.at[j, part], ss_a.at[0, 0, h], rs_a.at[j, h], dev(dc=0, dk=1)).wait_recv()

    def x0_copy(d):
        return copy(b_ref, bbuf.at[0, d, 0], ss_x0.at[d - 1], rs_x0.at[d - 1], dev(dx=-d))

    def k0_copy(d):
        src = b_ref if d == 0 else bbuf.at[0, d, 0]
        return copy(src, bbuf.at[0, d, 1], ss_k0.at[d], rs_k0.at[d], dev(dk=1))

    wb = 4 // HB

    def z_copy(h):
        part = pl.ds(h * wb, wb)
        return copy(b_ref.at[part], bbuf.at[1, 0, 0, part], ss_z.at[h], rs_z.at[h], dev(dz=1))

    def x1_copy(d, h):
        part = pl.ds(h * wb, wb)
        return copy(
            bbuf.at[1, 0, 0, part], bbuf.at[1, d, 0, part], ss_x1.at[d - 1, h], rs_x1.at[d - 1, h], dev(dx=-d)
        )

    def k1_copy(d, h):
        part = pl.ds(h * wb, wb)
        return copy(bbuf.at[1, d, 0, part], bbuf.at[1, d, 1, part], ss_k1.at[d, h], rs_k1.at[d, h], dev(dk=1))

    def c_copy(d):
        return copy(sbuf.at[d - 1], rbuf.at[d - 1], ss_c.at[d - 1], rs_c.at[d - 1], dev(dy=d))

    def each_a(t, h, act):
        @pl.when((c - t >= 0) & (c < NC - 1))
        def _():
            act(a_copy(1, t, h))

        @pl.when((c + t <= NC - 1) & (c > 0))
        def _():
            act(a_copy(-1, t, h))

    for h in range(HA):
        each_a(0, h, lambda cp: cp.start())
    for d in (2, 1, 3):
        x0_copy(d).start()
    k0_copy(0).start()

    def start_z(t):
        for core in range(2):
            if B_START[core] == t:
                @pl.when(k == core)
                def _():
                    for h in range(HB):
                        z_copy(h).start()

    start_z(0)

    def step_of(i):
        dz, dx, dk = i // 8, (i // 2) % 4, i % 2
        return ((x + dx) % NX) * 4 + ((zh + dz) % 2) * 2 + (k + dk) % 2

    def chain(i, heads):
        s = step_of(i)
        count = live[s]
        for t in range(TCAP):
            q = trip[s, t, 2]
            before = jnp.int32(STEPS * TCAP)
            for n in range(SLOTS):
                before = jnp.where(q == n, heads[n], before)
            prev[i * TCAP + t] = before
            here = jnp.where(t < count, q, SLOTS)
            heads = tuple(jnp.where(here == n, i * TCAP + t, heads[n]) for n in range(SLOTS))
        return heads

    none = jnp.int32(STEPS * TCAP)
    heads = lax.fori_loop(0, STEPS, chain, (none,) * SLOTS)
    for n in range(SLOTS):
        last[n] = heads[n]
    cum[STEPS * TCAP] = jnp.zeros((128, 128), jnp.float32)

    def split_a(j, src):
        for n in range(4):
            ahl[j * 4 + n] = split_pair(src(n))

    split_a(c, lambda n: a_ref[n])

    def split_b(i, src):
        for n in range(4):
            bhl[i * 4 + n] = split_pair(src(n))

    split_b(0, lambda n: b_ref[n])

    for t in range(1, NC):
        for h in range(HA):
            @pl.when(c - t >= 0)
            def _():
                a_arrived(c - t, h)

            @pl.when(c + t <= NC - 1)
            def _():
                a_arrived(c + t, h)

            each_a(t, h, lambda cp: cp.start())

        start_z(t)

        @pl.when(c - t >= 0)
        def _():
            split_a(c - t, lambda n: abuf[c - t, n])

        @pl.when(c + t <= NC - 1)
        def _():
            split_a(c + t, lambda n: abuf[c + t, n])

        if t <= 3:
            d = (1, 3, 2)[t - 1]
            x0_copy(d).wait_recv()
            k0_copy(d).start()
            split_b(d * 2, lambda n: bbuf[0, d, 0, n])

    def products(i):
        s = step_of(i)

        def one(t, carry):
            left = ahl[trip[s, t, 0]]
            right = bhl[i * 4 + trip[s, t, 1]]
            both = jnp.dot(
                left, jnp.concatenate([right, right], axis=0), preferred_element_type=jnp.float32
            )
            cum[i * TCAP + t] = cum[prev[i * TCAP + t]] + (both[:, :128] + both[:, 128:])
            return carry

        lax.fori_loop(0, TCAP, one, 0, unroll=4)

    for d in range(4):
        k0_copy(d).wait_recv()
        split_b(d * 2 + 1, lambda n: bbuf[0, d, 1, n])

    def group(i, carry):
        products(i)
        return carry

    lax.fori_loop(0, 8, group, 0)

    for h in range(HB):
        z_copy(h).wait_recv()
        for d in (2, 1, 3):
            x1_copy(d, h).start()
        k1_copy(0, h).start()
        for d in (1, 3, 2):
            x1_copy(d, h).wait_recv()
            k1_copy(d, h).start()
    for d in range(4):
        split_b(8 + d * 2, lambda n: bbuf[1, d, 0, n])
    for d in range(4):
        for h in range(HB):
            k1_copy(d, h).wait_recv()
        split_b(8 + d * 2 + 1, lambda n: bbuf[1, d, 1, n])

    lax.fori_loop(8, 16, group, 0)

    for d in (2, 1, 3):
        owner = (y + d) % NY
        for n in range(OWN):
            sbuf[d - 1, n] = cum[last[order[owner * OWN + n]]]
        c_copy(d).start()
    for n in range(OWN):
        out[n] = cum[last[order[y * OWN + n]]]
    for d in (1, 3, 2):
        c_copy(d).wait_recv()
        out[...] += rbuf[d - 1]

    for h in range(HA):
        for t in range(NC):
            each_a(t, h, lambda cp: cp.wait_send())
    for d in range(1, 4):
        x0_copy(d).wait_send()
        c_copy(d).wait_send()
        for h in range(HB):
            x1_copy(d, h).wait_send()
    for h in range(HB):
        z_copy(h).wait_send()
    for d in range(4):
        k0_copy(d).wait_send()
        for h in range(HB):
            k1_copy(d, h).wait_send()


def on_device(a_blocks, b_blocks, triples, live, c_order):
    f32, bf16 = jnp.float32, jnp.bfloat16
    vmem, smem = pl.BlockSpec(memory_space=pltpu.VMEM), pl.BlockSpec(memory_space=pltpu.SMEM)
    dma = pltpu.SemaphoreType.DMA
    result = pl.pallas_call(
        kernel,
        out_shape=jax.ShapeDtypeStruct((OWN, 128, 128), f32),
        in_specs=[vmem, vmem, smem, smem, smem],
        out_specs=vmem,
        scratch_shapes=[
            pltpu.VMEM((NC, 4, 128, 128), f32),
            pltpu.VMEM((2, 4, 2, 4, 128, 128), f32),
            pltpu.VMEM((NC * 4, 128, 256), bf16),
            pltpu.VMEM((STEPS * 4, 128, 256), bf16),
            pltpu.VMEM((STEPS * TCAP + 1, 128, 128), f32),
            pltpu.VMEM((3, OWN, 128, 128), f32),
            pltpu.VMEM((3, OWN, 128, 128), f32),
            pltpu.SMEM((STEPS * TCAP,), jnp.int32),
            pltpu.SMEM((SLOTS,), jnp.int32),
            dma((2, NC, HA)), dma((NC, HA)),
            dma((3,)), dma((3,)), dma((4,)), dma((4,)),
            dma((HB,)), dma((HB,)), dma((3, HB)), dma((3, HB)), dma((4, HB)), dma((4, HB)),
            dma((3,)), dma((3,)),
        ],
        compiler_params=pltpu.CompilerParams(
            collective_id=0, has_side_effects=True, vmem_limit_bytes=56 * 1024 * 1024
        ),
        name="block_sparse_product",
    )(a_blocks[0, 0, 0], b_blocks[0, 0, 0], triples[0, 0, 0], live[0, 0, 0], c_order[0, 0])
    return result.reshape(1, 1, 1, OWN, 128, 128)


def solution(mesh):
    placed = (
        P("row", "col", "depth", None, None, None),
        P("row", "col", "depth", None, None, None),
        P("row", "col", "depth", None, None, None),
        P("row", "col", "depth", None),
        P("row", "col", None),
    )
    return jax.shard_map(
        on_device,
        mesh=mesh,
        in_specs=placed,
        out_specs=P("row", "col", "depth", None, None, None),
        check_vma=False,
    )
```

time: 433 us -> 142 us (0.33)
  waiting for transfers between devices: 249 us -> 0 us
  Pallas kernels: 0 us -> 138 us
  matrix products: 78.5 us -> 0 us
  local copies, waits for them, and re-layouts: 76.6 us -> 3.23 us
  between operations: 13.1 us -> 0.01 us
  other arithmetic: 12.1 us -> 0 us
    all_gather x2 -> x0, waiting for transfers between devices: 196 us -> none  [the longest x1 124 us: on_device(): pieces = lax.all_gather(b_blocks, 'row', axis=0, tiled=True)]
    pallas_call x0 -> x1, Pallas kernels: none -> 138 us  [on_device(): pl.pallas_call(kernel, out_shape=jax.ShapeDtypeStruct((OWN, 128, 128), f3...]
    dot_general x32 -> x0, matrix products: 78.5 us -> none  [the longest x16 58.2 us: block_products(): jnp.einsum('ct,tij->cij', placing, products, precision=lax.Precision.HIGH...]
    psum x1 -> x0, waiting for transfers between devices: 52.3 us -> none  [on_device(): summed_all = lax.psum(partial_sum, 'depth')]
    gather x33 -> x0, local copies, waits for them, and re-layouts: 46.9 us -> none  [the longest x16 35.3 us: block_products(): left_blocks = jnp.take(a_panel, triple_rows[:, 0], axis=0)]
    squeeze x32 -> x0, local copies, waits for them, and re-layouts: 15.9 us -> none  [the longest x16 15.7 us: one_step(): b_shard = lax.dynamic_index_in_dim(shards, offset, 0, keepdims=False)]
    convert_element_type x16 -> x0, other arithmetic: 10.8 us -> none  [block_products(): (jnp.arange(width, dtype=jnp.int32) < live_count).astype(jnp.float32)]
    dynamic_slice x16 -> x0, local copies, waits for them, and re-layouts: 10.4 us -> none  [one_step(): live_count = lax.dynamic_index_in_dim(live_table, offset, 0, keepdims=False)]
  transfers between devices with their start and end apart: 3 -> 0, of which waited for: 3 -> 0; matrix products, arithmetic and copies ran while one was open for 0% -> 0% of each run, Pallas kernels for 0% -> 0%
where the time goes in v1:
time: 142 us
  Pallas kernels  138 us (97%)
  local copies, waits for them, and re-layouts  3.23 us (2%)
    pallas_call x1, Pallas kernels, on_device(): pl.pallas_call(kernel, out_shape=jax.ShapeDtypeStruct((OWN, 128, 128), f3...  138 us
    unnamed x2, local copies, waits for them, and re-layouts  3.23 us

profile of v1, /device:TPU:1, one launch (start us, length us, event | category | flops | bytes accessed | tf_op | source)
XLA Modules:
  0.0 141.6 jit_solution(11843766064900406640)
XLA Ops:
  0.0 1.6 %copy.6 = s32[1,1,1,16,16,3]{5,4,3,2,1,0:T(8,128)} copy(s32[1,1,1,16,16,3]{4,3,5,2,1,0:T(8,128)} %param.7) | data formatting | bytes 6144 | tf_op args[2]
  1.6 138.4 %block_sparse_product.1 = f32[4,128,128]{2,1,0:T(8,128)} custom-call(f32[4,128,128]{2,1,0:T(8,128)} %bitcast.8, f32[4,128,128]{2,1,0:T(8,128)} %bitcast.9, s32[16,16,3]{2,1,0:T(8,128)} %bitcast.7, s32[16]{0:T(128)} %bitcast.10, s32[16]{0:T(128)} %bitcast.11), custom_call_target="tpu_custom_call" | custom-call | tf_op jit(solution)/shard_map/block_sparse_product/pallas_call | solution.py:256
  140.0 1.7 %copy.8 = f32[1,1,1,4,128,128]{5,4,3,2,1,0:T(8,128)} copy(f32[1,1,1,4,128,128]{5,4,3,2,1,0:T(8,128)} %bitcast.6) | data formatting | bytes 524288

commit v2 on v1

--- a/solution.py
+++ b/solution.py
@@ -10,8 +10,9 @@
 MESH = pl.DeviceIdType.MESH
 NX, NY, NZ, NC = 4, 4, 16, 8
 STEPS, TCAP, SLOTS, OWN = 16, 16, 16, 4
-HA, HB = 2, 4
-B_START = (2, 4)
+HA = 2
+WINDOW = 2
+UNROLL = 16
 
 
 def split_pair(block):
@@ -22,7 +23,7 @@
 
 def kernel(
     a_ref, b_ref, trip, live, order, out,
-    abuf, bbuf, ahl, bhl, cum, sbuf, rbuf, prev, last,
+    abuf, bbuf, ahl, bhl, cum, sbuf, via, rbuf, prev, last,
     ss_a, rs_a, ss_x0, rs_x0, ss_k0, rs_k0, ss_z, rs_z, ss_x1, rs_x1, ss_k1, rs_k1, ss_c, rs_c,
 ):
     row, c, y = lax.axis_index("row"), lax.axis_index("col"), lax.axis_index("depth")
@@ -38,7 +39,7 @@
         )
 
     barrier = pltpu.get_barrier_semaphore()
-    partners = [dev(dx=1), dev(dx=2), dev(dx=3), dev(dz=1), dev(dk=1), dev(dy=1), dev(dy=2), dev(dy=3)]
+    partners = [dev(dx=1), dev(dx=2), dev(dx=3), dev(dz=1), dev(dk=1), dev(dy=1), dev(dy=-1)]
     for p in partners:
         pl.semaphore_signal(barrier, inc=1, device_id=p, device_id_type=MESH)
 
@@ -74,49 +75,57 @@
         src = b_ref if d == 0 else bbuf.at[0, d, 0]
         return copy(src, bbuf.at[0, d, 1], ss_k0.at[d], rs_k0.at[d], dev(dk=1))
 
-    wb = 4 // HB
-
-    def z_copy(h):
-        part = pl.ds(h * wb, wb)
-        return copy(b_ref.at[part], bbuf.at[1, 0, 0, part], ss_z.at[h], rs_z.at[h], dev(dz=1))
-
-    def x1_copy(d, h):
-        part = pl.ds(h * wb, wb)
+    def z_copy():
+        return copy(b_ref, bbuf.at[1, 0, 0], ss_z.at[0], rs_z.at[0], dev(dz=1))
+
+    def x1_copy(d):
+        return copy(bbuf.at[1, 0, 0], bbuf.at[1, d, 0], ss_x1.at[d - 1], rs_x1.at[d - 1], dev(dx=-d))
+
+    def k1_copy(d):
+        return copy(bbuf.at[1, d, 0], bbuf.at[1, d, 1], ss_k1.at[d], rs_k1.at[d], dev(dk=1))
+
+    def c_copy(side, stage):
+        keep = pl.ds(2 * (side if stage == 2 else 1 - side), 2)
+        dst = via.at[side] if stage == 0 else rbuf.at[side, keep]
         return copy(
-            bbuf.at[1, 0, 0, part], bbuf.at[1, d, 0, part], ss_x1.at[d - 1, h], rs_x1.at[d - 1, h], dev(dx=-d)
+            sbuf.at[side, stage], dst, ss_c.at[side, stage], rs_c.at[side, stage], dev(dy=1 - 2 * side)
         )
 
-    def k1_copy(d, h):
-        part = pl.ds(h * wb, wb)
-        return copy(bbuf.at[1, d, 0, part], bbuf.at[1, d, 1, part], ss_k1.at[d, h], rs_k1.at[d, h], dev(dk=1))
-
-    def c_copy(d):
-        return copy(sbuf.at[d - 1], rbuf.at[d - 1], ss_c.at[d - 1], rs_c.at[d - 1], dev(dy=d))
-
-    def each_a(t, h, act):
-        @pl.when((c - t >= 0) & (c < NC - 1))
+    def each_a(n, act, done=False):
+        t, h = divmod(n, HA)
+        last_of = (n + WINDOW) // HA
+        right, left = (c - t >= 0) & (c < NC - 1), (c + t <= NC - 1) & (c > 0)
+        if done:
+            right, left = right & (c - last_of < 0), left & (c + last_of > NC - 1)
+
+        @pl.when(right)
         def _():
             act(a_copy(1, t, h))
 
-        @pl.when((c + t <= NC - 1) & (c > 0))
+        @pl.when(left)
         def _():
             act(a_copy(-1, t, h))
 
+    def send_a(n):
+        t, h = divmod(n, HA)
+        if n >= WINDOW:
+            to, ho = divmod(n - WINDOW, HA)
+
+            @pl.when((c - t >= 0) & (c < NC - 1))
+            def _():
+                a_copy(1, to, ho).wait_send()
+
+            @pl.when((c + t <= NC - 1) & (c > 0))
+            def _():
+                a_copy(-1, to, ho).wait_send()
+        each_a(n, lambda cp: cp.start())
+
+    z_copy().start()
     for h in range(HA):
-        each_a(0, h, lambda cp: cp.start())
+        send_a(h)
     for d in (2, 1, 3):
         x0_copy(d).start()
     k0_copy(0).start()
-
-    def start_z(t):
-        for core in range(2):
-            if B_START[core] == t:
-                @pl.when(k == core)
-                def _():
-                    for h in range(HB):
-                        z_copy(h).start()
-
-    start_z(0)
 
     def step_of(i):
         dz, dx, dk = i // 8, (i // 2) % 4, i % 2
@@ -126,7 +135,7 @@
         s = step_of(i)
         count = live[s]
         for t in range(TCAP):
-            q = trip[s, t, 2]
+            q = trip[2, s, t]
             before = jnp.int32(STEPS * TCAP)
             for n in range(SLOTS):
                 before = jnp.where(q == n, heads[n], before)
@@ -153,6 +162,12 @@
 
     split_b(0, lambda n: b_ref[n])
 
+    z_copy().wait_recv()
+    for d in (2, 1, 3):
+        x1_copy(d).start()
+    k1_copy(0).start()
+    split_b(8, lambda n: bbuf[1, 0, 0, n])
+
     for t in range(1, NC):
         for h in range(HA):
             @pl.when(c - t >= 0)
@@ -163,9 +178,7 @@
             def _():
                 a_arrived(c + t, h)
 
-            each_a(t, h, lambda cp: cp.start())
-
-        start_z(t)
+            send_a(t * HA + h)
 
         @pl.when(c - t >= 0)
         def _():
@@ -180,73 +193,72 @@
             x0_copy(d).wait_recv()
             k0_copy(d).start()
             split_b(d * 2, lambda n: bbuf[0, d, 0, n])
-
-    def products(i):
+        if 2 <= t <= 4:
+            d = (1, 3, 2)[t - 2]
+            x1_copy(d).wait_recv()
+            k1_copy(d).start()
+            split_b(8 + d * 2, lambda n: bbuf[1, d, 0, n])
+        if 4 <= t:
+            d = t - 4
+            k0_copy(d).wait_recv()
+            split_b(d * 2 + 1, lambda n: bbuf[0, d, 1, n])
+            k1_copy(d).wait_recv()
+            split_b(8 + d * 2 + 1, lambda n: bbuf[1, d, 1, n])
+
+    def products(i, carry):
         s = step_of(i)
 
         def one(t, carry):
-            left = ahl[trip[s, t, 0]]
-            right = bhl[i * 4 + trip[s, t, 1]]
+            left = ahl[trip[0, s, t]]
+            right = bhl[i * 4 + trip[1, s, t]]
             both = jnp.dot(
                 left, jnp.concatenate([right, right], axis=0), preferred_element_type=jnp.float32
             )
             cum[i * TCAP + t] = cum[prev[i * TCAP + t]] + (both[:, :128] + both[:, 128:])
             return carry
 
-        lax.fori_loop(0, TCAP, one, 0, unroll=4)
-
-    for d in range(4):
-        k0_copy(d).wait_recv()
-        split_b(d * 2 + 1, lambda n: bbuf[0, d, 1, n])
-
-    def group(i, carry):
-        products(i)
-        return carry
-
-    lax.fori_loop(0, 8, group, 0)
-
-    for h in range(HB):
-        z_copy(h).wait_recv()
-        for d in (2, 1, 3):
-            x1_copy(d, h).start()
-        k1_copy(0, h).start()
-        for d in (1, 3, 2):
-            x1_copy(d, h).wait_recv()
-            k1_copy(d, h).start()
-    for d in range(4):
-        split_b(8 + d * 2, lambda n: bbuf[1, d, 0, n])
-    for d in range(4):
-        for h in range(HB):
-            k1_copy(d, h).wait_recv()
-        split_b(8 + d * 2 + 1, lambda n: bbuf[1, d, 1, n])
-
-    lax.fori_loop(8, 16, group, 0)
-
-    for d in (2, 1, 3):
-        owner = (y + d) % NY
-        for n in range(OWN):
-            sbuf[d - 1, n] = cum[last[order[owner * OWN + n]]]
-        c_copy(d).start()
+        return lax.fori_loop(0, TCAP, one, carry, unroll=UNROLL)
+
+    lax.fori_loop(0, STEPS, products, 0)
+
+    def total(owner, n):
+        return cum[last[order[((y + owner + NY) % NY) * OWN + n]]]
+
+    for stage in (0, 1):
+        for side in (0, 1):
+            for n in range(2):
+                if stage == 0:
+                    sbuf[side, 0, n] = total(2, 2 * side + n)
+                else:
+                    sbuf[side, 1, n] = total(1 - 2 * side, 2 * (1 - side) + n)
+            c_copy(side, stage).start()
+    for side in (0, 1):
+        for n in range(2):
+            sbuf[side, 2, n] = total(1 - 2 * side, 2 * side + n)
     for n in range(OWN):
-        out[n] = cum[last[order[y * OWN + n]]]
-    for d in (1, 3, 2):
-        c_copy(d).wait_recv()
-        out[...] += rbuf[d - 1]
-
-    for h in range(HA):
-        for t in range(NC):
-            each_a(t, h, lambda cp: cp.wait_send())
+        out[n] = total(0, n)
+    for side in (0, 1):
+        c_copy(side, 0).wait_recv()
+        sbuf[side, 2] += via[side]
+        c_copy(side, 2).start()
+    for stage in (1, 2):
+        for side in (0, 1):
+            c_copy(side, stage).wait_recv()
+            keep = pl.ds(2 * (side if stage == 2 else 1 - side), 2)
+            out[keep] += rbuf[side, keep]
+
+    for n in range(NC * HA):
+        each_a(n, lambda cp: cp.wait_send(), done=True)
+    z_copy().wait_send()
     for d in range(1, 4):
         x0_copy(d).wait_send()
-        c_copy(d).wait_send()
-        for h in range(HB):
-            x1_copy(d, h).wait_send()
-    for h in range(HB):
-        z_copy(h).wait_send()
+        x1_copy(d).wait_send()
     for d in range(4):
         k0_copy(d).wait_send()
-        for h in range(HB):
-            k1_copy(d, h).wait_send()
+        k1_copy(d).wait_send()
+    for side in (0, 1):
+        for stage in range(3):
+            c_copy(side, stage).wait_send()
 
 
 def on_device(a_blocks, b_blocks, triples, live, c_order):
@@ -264,20 +276,21 @@
             pltpu.VMEM((NC * 4, 128, 256), bf16),
             pltpu.VMEM((STEPS * 4, 128, 256), bf16),
             pltpu.VMEM((STEPS * TCAP + 1, 128, 128), f32),
-            pltpu.VMEM((3, OWN, 128, 128), f32),
-            pltpu.VMEM((3, OWN, 128, 128), f32),
+            pltpu.VMEM((2, 3, 2, 128, 128), f32),
+            pltpu.VMEM((2, 2, 128, 128), f32),
+            pltpu.VMEM((2, OWN, 128, 128), f32),
             pltpu.SMEM((STEPS * TCAP,), jnp.int32),
             pltpu.SMEM((SLOTS,), jnp.int32),
             dma((2, NC, HA)), dma((NC, HA)),
             dma((3,)), dma((3,)), dma((4,)), dma((4,)),
-            dma((HB,)), dma((HB,)), dma((3, HB)), dma((3, HB)), dma((4, HB)), dma((4, HB)),
-            dma((3,)), dma((3,)),
+            dma((1,)), dma((1,)), dma((3,)), dma((3,)), dma((4,)), dma((4,)),
+            dma((2, 3)), dma((2, 3)),
         ],
         compiler_params=pltpu.CompilerParams(
             collective_id=0, has_side_effects=True, vmem_limit_bytes=56 * 1024 * 1024
         ),
         name="block_sparse_product",
-    )(a_blocks[0, 0, 0], b_blocks[0, 0, 0], triples[0, 0, 0], live[0, 0, 0], c_order[0, 0])
+    )(a_blocks[0, 0, 0], b_blocks[0, 0, 0], jnp.transpose(triples[0, 0, 0], (2, 0, 1)), live[0, 0, 0], c_order[0, 0])
     return result.reshape(1, 1, 1, OWN, 128, 128)
 
 

time: 142 us -> 102 us (0.72)
  Pallas kernels: 138 us -> 99.2 us
  local copies, waits for them, and re-layouts: 3.23 us -> 1.67 us
    pallas_call x1, Pallas kernels: 138 us -> 99.2 us  [on_device(): pl.pallas_call(kernel, out_shape=jax.ShapeDtypeStruct((OWN, 128, 128), f3...]
    unnamed x2 -> x1, local copies, waits for them, and re-layouts: 3.23 us -> 1.67 us
where the time goes in v2:
time: 102 us; the launch traced here: 101 us
  Pallas kernels  99.2 us (97%)
  local copies, waits for them, and re-layouts  1.67 us (2%)
    pallas_call x1, Pallas kernels, on_device(): pl.pallas_call(kernel, out_shape=jax.ShapeDtypeStruct((OWN, 128, 128), f3...  99.2 us

profile of v2, /device:TPU:1, one launch (start us, length us, event | category | flops | bytes accessed | tf_op | source)
XLA Modules:
  0.0 100.9 jit_solution(5063142023171699539)
XLA Ops:
  0.0 99.2 %block_sparse_product.1 = f32[4,128,128]{2,1,0:T(8,128)} custom-call(f32[4,128,128]{2,1,0:T(8,128)} %bitcast.9, f32[4,128,128]{2,1,0:T(8,128)} %bitcast.10, s32[3,16,16]{2,1,0:T(8,128)} %bitcast.11, s32[16]{0:T(128)} %bitcast.12, s32[16]{0:T(128)} %bitcast.13), custom_call_target="tpu_custom_call" | custom-call | tf_op jit(solution)/shard_map/block_sparse_product/pallas_call | solution.py:268
  99.2 1.7 %copy.7 = f32[1,1,1,4,128,128]{5,4,3,2,1,0:T(8,128)} copy(f32[1,1,1,4,128,128]{5,4,3,2,1,0:T(8,128)} %bitcast.8) | data formatting | bytes 524288

commit v3 on v2

--- a/solution.py
+++ b/solution.py
@@ -9,10 +9,10 @@
 
 MESH = pl.DeviceIdType.MESH
 NX, NY, NZ, NC = 4, 4, 16, 8
-STEPS, TCAP, SLOTS, OWN = 16, 16, 16, 4
+STEPS, TCAP, SLOTS, BSL, OWN = 16, 16, 16, 4, 4
 HA = 2
 WINDOW = 2
-UNROLL = 16
+UNROLL = 64
 
 
 def split_pair(block):
@@ -23,7 +23,7 @@
 
 def kernel(
     a_ref, b_ref, trip, live, order, out,
-    abuf, bbuf, ahl, bhl, cum, sbuf, via, rbuf, prev, last,
+    abuf, bbuf, ahl, bhl, cum, sbuf, via, rbuf, prev, lefts, rights, last,
     ss_a, rs_a, ss_x0, rs_x0, ss_k0, rs_k0, ss_z, rs_z, ss_x1, rs_x1, ss_k1, rs_k1, ss_c, rs_c,
 ):
     row, c, y = lax.axis_index("row"), lax.axis_index("col"), lax.axis_index("depth")
@@ -39,20 +39,25 @@
         )
 
     barrier = pltpu.get_barrier_semaphore()
-    partners = [dev(dx=1), dev(dx=2), dev(dx=3), dev(dz=1), dev(dk=1), dev(dy=1), dev(dy=-1)]
+
+    def greet(to):
+        pl.semaphore_signal(barrier, inc=1, device_id=to, device_id_type=MESH)
+
+    partners = [dev(dx=1), dev(dx=2), dev(dx=3), dev(dk=1), dev(dy=1), dev(dy=-1)]
     for p in partners:
-        pl.semaphore_signal(barrier, inc=1, device_id=p, device_id_type=MESH)
+        greet(p)
 
     @pl.when(c > 0)
     def _():
-        pl.semaphore_signal(barrier, inc=1, device_id=dev(dc=-1), device_id_type=MESH)
+        greet(dev(dc=-1))
 
     @pl.when(c < NC - 1)
     def _():
-        pl.semaphore_signal(barrier, inc=1, device_id=dev(dc=1), device_id_type=MESH)
+        greet(dev(dc=1))
 
     ends = (c > 0).astype(jnp.int32) + (c < NC - 1).astype(jnp.int32)
-    pl.semaphore_wait(barrier, len(partners) + ends)
+    pl.semaphore_wait(barrier, len(partners) + ends + zh)
+    greet(dev(dz=1))
 
     wa = 4 // HA
 
@@ -120,12 +125,20 @@
                 a_copy(-1, to, ho).wait_send()
         each_a(n, lambda cp: cp.start())
 
-    z_copy().start()
+    @pl.when(zh == 1)
+    def _():
+        z_copy().start()
+
     for h in range(HA):
         send_a(h)
     for d in (2, 1, 3):
         x0_copy(d).start()
     k0_copy(0).start()
+
+    @pl.when(zh == 0)
+    def _():
+        pl.semaphore_wait(barrier, 1)
+        z_copy().start()
 
     def step_of(i):
         dz, dx, dk = i // 8, (i // 2) % 4, i % 2
@@ -140,6 +153,8 @@
             for n in range(SLOTS):
                 before = jnp.where(q == n, heads[n], before)
             prev[i * TCAP + t] = before
+            lefts[i * TCAP + t] = trip[0, s, t]
+            rights[i * TCAP + t] = i * BSL + trip[1, s, t]
             here = jnp.where(t < count, q, SLOTS)
             heads = tuple(jnp.where(here == n, i * TCAP + t, heads[n]) for n in range(SLOTS))
         return heads
@@ -205,21 +220,15 @@
             k1_copy(d).wait_recv()
             split_b(8 + d * 2 + 1, lambda n: bbuf[1, d, 1, n])
 
-    def products(i, carry):
-        s = step_of(i)
-
-        def one(t, carry):
-            left = ahl[trip[0, s, t]]
-            right = bhl[i * 4 + trip[1, s, t]]
-            both = jnp.dot(
-                left, jnp.concatenate([right, right], axis=0), preferred_element_type=jnp.float32
-            )
-            cum[i * TCAP + t] = cum[prev[i * TCAP + t]] + (both[:, :128] + both[:, 128:])
-            return carry
-
-        return lax.fori_loop(0, TCAP, one, carry, unroll=UNROLL)
-
-    lax.fori_loop(0, STEPS, products, 0)
+    def product(i, carry):
+        right = bhl[rights[i]]
+        both = jnp.dot(
+            ahl[lefts[i]], jnp.concatenate([right, right], axis=0), preferred_element_type=jnp.float32
+        )
+        cum[i] = cum[prev[i]] + (both[:, :128] + both[:, 128:])
+        return carry
+
+    lax.fori_loop(0, STEPS * TCAP, product, 0, unroll=UNROLL)
 
     def total(owner, n):
         return cum[last[order[((y + owner + NY) % NY) * OWN + n]]]
@@ -280,6 +289,8 @@
             pltpu.VMEM((2, 2, 128, 128), f32),
             pltpu.VMEM((2, OWN, 128, 128), f32),
             pltpu.SMEM((STEPS * TCAP,), jnp.int32),
+            pltpu.SMEM((STEPS * TCAP,), jnp.int32),
+            pltpu.SMEM((STEPS * TCAP,), jnp.int32),
             pltpu.SMEM((SLOTS,), jnp.int32),
             dma((2, NC, HA)), dma((NC, HA)),
             dma((3,)), dma((3,)), dma((4,)), dma((4,)),

time: 102 us -> 97.9 us (0.960)
  Pallas kernels: 99.2 us -> 96 us
    pallas_call x1, Pallas kernels: 99.2 us -> 96 us  [on_device(): pl.pallas_call(kernel, out_shape=jax.ShapeDtypeStruct((OWN, 128, 128), f3...]
where the time goes in v3:
time: 97.9 us; the launch traced here: 97.7 us
  Pallas kernels  96 us (98%)
  local copies, waits for them, and re-layouts  1.67 us (2%)
    pallas_call x1, Pallas kernels, on_device(): pl.pallas_call(kernel, out_shape=jax.ShapeDtypeStruct((OWN, 128, 128), f3...  96 us

profile of v3, /device:TPU:1, one launch (start us, length us, event | category | flops | bytes accessed | tf_op | source)
XLA Modules:
  0.0 97.7 jit_solution(3583756658085784121)
XLA Ops:
  0.0 96.0 %block_sparse_product.1 = f32[4,128,128]{2,1,0:T(8,128)} custom-call(f32[4,128,128]{2,1,0:T(8,128)} %bitcast.9, f32[4,128,128]{2,1,0:T(8,128)} %bitcast.10, s32[3,16,16]{2,1,0:T(8,128)} %bitcast.11, s32[16]{0:T(128)} %bitcast.12, s32[16]{0:T(128)} %bitcast.13), custom_call_target="tpu_custom_call" | custom-call | tf_op jit(solution)/shard_map/block_sparse_product/pallas_call | solution.py:277
  96.0 1.7 %copy.7 = f32[1,1,1,4,128,128]{5,4,3,2,1,0:T(8,128)} copy(f32[1,1,1,4,128,128]{5,4,3,2,1,0:T(8,128)} %bitcast.8) | data formatting | bytes 524288

commit v4 on v3

--- a/solution.py
+++ b/solution.py
@@ -13,6 +13,7 @@
 HA = 2
 WINDOW = 2
 UNROLL = 64
+Z_WAIT, FAR_WAIT = 2, 1
 
 
 def split_pair(block):
@@ -125,20 +126,21 @@
                 a_copy(-1, to, ho).wait_send()
         each_a(n, lambda cp: cp.start())
 
+    for h in range(HA):
+        send_a(h)
+
     @pl.when(zh == 1)
     def _():
         z_copy().start()
-
-    for h in range(HA):
-        send_a(h)
     for d in (2, 1, 3):
         x0_copy(d).start()
     k0_copy(0).start()
 
-    @pl.when(zh == 0)
-    def _():
-        pl.semaphore_wait(barrier, 1)
-        z_copy().start()
+    def hear_far():
+        @pl.when(zh == 0)
+        def _():
+            pl.semaphore_wait(barrier, 1)
+            z_copy().start()
 
     def step_of(i):
         dz, dx, dk = i // 8, (i // 2) % 4, i % 2
@@ -177,11 +179,39 @@
 
     split_b(0, lambda n: b_ref[n])
 
-    z_copy().wait_recv()
-    for d in (2, 1, 3):
-        x1_copy(d).start()
-    k1_copy(0).start()
-    split_b(8, lambda n: bbuf[1, 0, 0, n])
+    def forward_z():
+        z_copy().wait_recv()
+        for d in (2, 1, 3):
+            x1_copy(d).start()
+        k1_copy(0).start()
+        split_b(8, lambda n: bbuf[1, 0, 0, n])
+
+    def forward_x0(d):
+        x0_copy(d).wait_recv()
+        k0_copy(d).start()
+        split_b(d * 2, lambda n: bbuf[0, d, 0, n])
+
+    def forward_x1(d):
+        x1_copy(d).wait_recv()
+        k1_copy(d).start()
+        split_b(8 + d * 2, lambda n: bbuf[1, d, 0, n])
+
+    def take_k0(d):
+        k0_copy(d).wait_recv()
+        split_b(d * 2 + 1, lambda n: bbuf[0, d, 1, n])
+
+    def take_k1(d):
+        k1_copy(d).wait_recv()
+        split_b(8 + d * 2 + 1, lambda n: bbuf[1, d, 1, n])
+
+    jobs = {t: [] for t in range(NC + 3)}
+    jobs[Z_WAIT].append(forward_z)
+    for n, d in enumerate((1, 3, 2)):
+        jobs[1 + n].append(functools.partial(forward_x0, d))
+        jobs[Z_WAIT + 2 + n].append(functools.partial(forward_x1, d))
+    for n, d in enumerate((0, 1, 3, 2)):
+        jobs[4 + n].append(functools.partial(take_k0, d))
+        jobs[Z_WAIT + 3 + n].append(functools.partial(take_k1, d))
 
     for t in range(1, NC):
         for h in range(HA):
@@ -203,22 +233,13 @@
         def _():
             split_a(c + t, lambda n: abuf[c + t, n])
 
-        if t <= 3:
-            d = (1, 3, 2)[t - 1]
-            x0_copy(d).wait_recv()
-            k0_copy(d).start()
-            split_b(d * 2, lambda n: bbuf[0, d, 0, n])
-        if 2 <= t <= 4:
-            d = (1, 3, 2)[t - 2]
-            x1_copy(d).wait_recv()
-            k1_copy(d).start()
-            split_b(8 + d * 2, lambda n: bbuf[1, d, 0, n])
-        if 4 <= t:
-            d = t - 4
-            k0_copy(d).wait_recv()
-            split_b(d * 2 + 1, lambda n: bbuf[0, d, 1, n])
-            k1_copy(d).wait_recv()
-            split_b(8 + d * 2 + 1, lambda n: bbuf[1, d, 1, n])
+        if t == FAR_WAIT:
+            hear_far()
+        for job in jobs[t]:
+            job()
+    for t in range(NC, NC + 3):
+        for job in jobs[t]:
+            job()
 
     def product(i, carry):
         right = bhl[rights[i]]

time: 97.9 us -> 91.9 us (0.939); the launches traced: 97.7 us -> 90.2 us
  Pallas kernels: 96 us -> 88.5 us
    pallas_call x1, Pallas kernels: 96 us -> 88.5 us  [on_device(): pl.pallas_call(kernel, out_shape=jax.ShapeDtypeStruct((OWN, 128, 128), f3...]
where the time goes in v4:
time: 91.9 us; the launch traced here: 90.2 us
  Pallas kernels  88.5 us (96%)
  local copies, waits for them, and re-layouts  1.67 us (2%)
    pallas_call x1, Pallas kernels, on_device(): pl.pallas_call(kernel, out_shape=jax.ShapeDtypeStruct((OWN, 128, 128), f3...  88.5 us

profile of v4, /device:TPU:1, one launch (start us, length us, event | category | flops | bytes accessed | tf_op | source)
XLA Modules:
  0.0 90.2 jit_solution(14173630319327160250)
XLA Ops:
  0.0 88.5 %block_sparse_product.1 = f32[4,128,128]{2,1,0:T(8,128)} custom-call(f32[4,128,128]{2,1,0:T(8,128)} %bitcast.9, f32[4,128,128]{2,1,0:T(8,128)} %bitcast.10, s32[3,16,16]{2,1,0:T(8,128)} %bitcast.11, s32[16]{0:T(128)} %bitcast.12, s32[16]{0:T(128)} %bitcast.13), custom_call_target="tpu_custom_call" | custom-call | tf_op jit(solution)/shard_map/block_sparse_product/pallas_call | solution.py:298
  88.5 1.7 %copy.7 = f32[1,1,1,4,128,128]{5,4,3,2,1,0:T(8,128)} copy(f32[1,1,1,4,128,128]{5,4,3,2,1,0:T(8,128)} %bitcast.8) | data formatting | bytes 524288

commit v5 on v4

--- a/solution.py
+++ b/solution.py
@@ -97,37 +97,26 @@
             sbuf.at[side, stage], dst, ss_c.at[side, stage], rs_c.at[side, stage], dev(dy=1 - 2 * side)
         )
 
-    def each_a(n, act, done=False):
-        t, h = divmod(n, HA)
-        last_of = (n + WINDOW) // HA
-        right, left = (c - t >= 0) & (c < NC - 1), (c + t <= NC - 1) & (c > 0)
-        if done:
-            right, left = right & (c - last_of < 0), left & (c + last_of > NC - 1)
-
-        @pl.when(right)
-        def _():
-            act(a_copy(1, t, h))
-
-        @pl.when(left)
-        def _():
-            act(a_copy(-1, t, h))
-
-    def send_a(n):
-        t, h = divmod(n, HA)
-        if n >= WINDOW:
-            to, ho = divmod(n - WINDOW, HA)
-
-            @pl.when((c - t >= 0) & (c < NC - 1))
-            def _():
-                a_copy(1, to, ho).wait_send()
-
-            @pl.when((c + t <= NC - 1) & (c > 0))
-            def _():
-                a_copy(-1, to, ho).wait_send()
-        each_a(n, lambda cp: cp.start())
+    def sends(direction, t):
+        if direction == 1:
+            return (c - t >= 0) & (c < NC - 1)
+        return (c + t <= NC - 1) & (c > 0)
+
+    def send_a(direction, n):
+        @pl.when(sends(direction, n // HA))
+        def _():
+            if n >= WINDOW:
+                a_copy(direction, *divmod(n - WINDOW, HA)).wait_send()
+            a_copy(direction, *divmod(n, HA)).start()
+
+    def drain_a(direction, n):
+        @pl.when(sends(direction, n // HA) & jnp.logical_not(sends(direction, (n + WINDOW) // HA)))
+        def _():
+            a_copy(direction, *divmod(n, HA)).wait_send()
 
     for h in range(HA):
-        send_a(h)
+        for direction in (1, -1):
+            send_a(direction, h)
 
     @pl.when(zh == 1)
     def _():
@@ -208,22 +197,23 @@
     jobs[Z_WAIT].append(forward_z)
     for n, d in enumerate((1, 3, 2)):
         jobs[1 + n].append(functools.partial(forward_x0, d))
-        jobs[Z_WAIT + 2 + n].append(functools.partial(forward_x1, d))
+        jobs[Z_WAIT + 3 + n].append(functools.partial(forward_x1, d))
     for n, d in enumerate((0, 1, 3, 2)):
         jobs[4 + n].append(functools.partial(take_k0, d))
-        jobs[Z_WAIT + 3 + n].append(functools.partial(take_k1, d))
+        jobs[Z_WAIT + 4 + n].append(functools.partial(take_k1, d))
 
     for t in range(1, NC):
+        if t == NC - 1:
+            for later in range(t, NC + 3):
+                for job in jobs[later]:
+                    job()
         for h in range(HA):
-            @pl.when(c - t >= 0)
-            def _():
-                a_arrived(c - t, h)
-
-            @pl.when(c + t <= NC - 1)
-            def _():
-                a_arrived(c + t, h)
-
-            send_a(t * HA + h)
+            for direction in (1, -1):
+                @pl.when((c - t * direction >= 0) & (c - t * direction <= NC - 1))
+                def _():
+                    a_arrived(c - t * direction, h)
+
+                send_a(direction, t * HA + h)
 
         @pl.when(c - t >= 0)
         def _():
@@ -235,11 +225,9 @@
 
         if t == FAR_WAIT:
             hear_far()
-        for job in jobs[t]:
-            job()
-    for t in range(NC, NC + 3):
-        for job in jobs[t]:
-            job()
+        if t < NC - 1:
+            for job in jobs[t]:
+                job()
 
     def product(i, carry):
         right = bhl[rights[i]]
@@ -278,7 +266,8 @@
             out[keep] += rbuf[side, keep]
 
     for n in range(NC * HA):
-        each_a(n, lambda cp: cp.wait_send(), done=True)
+        drain_a(1, n)
+        drain_a(-1, n)
     z_copy().wait_send()
     for d in range(1, 4):
         x0_copy(d).wait_send()

time: 91.9 us -> 91.8 us (level)
  no operation moved by 1% of the time
where the time goes in v5:
time: 91.8 us; the launch traced here: 90.1 us
  Pallas kernels  88.4 us (96%)
  local copies, waits for them, and re-layouts  1.67 us (2%)
    pallas_call x1, Pallas kernels, on_device(): pl.pallas_call(kernel, out_shape=jax.ShapeDtypeStruct((OWN, 128, 128), f3...  88.4 us

profile of v5, /device:TPU:1, one launch (start us, length us, event | category | flops | bytes accessed | tf_op | source)
XLA Modules:
  0.0 90.1 jit_solution(10466951644173478638)
XLA Ops:
  0.0 88.4 %block_sparse_product.1 = f32[4,128,128]{2,1,0:T(8,128)} custom-call(f32[4,128,128]{2,1,0:T(8,128)} %bitcast.9, f32[4,128,128]{2,1,0:T(8,128)} %bitcast.10, s32[3,16,16]{2,1,0:T(8,128)} %bitcast.11, s32[16]{0:T(128)} %bitcast.12, s32[16]{0:T(128)} %bitcast.13), custom_call_target="tpu_custom_call" | custom-call | tf_op jit(solution)/shard_map/block_sparse_product/pallas_call | solution.py:287
  88.4 1.7 %copy.7 = f32[1,1,1,4,128,128]{5,4,3,2,1,0:T(8,128)} copy(f32[1,1,1,4,128,128]{5,4,3,2,1,0:T(8,128)} %bitcast.8) | data formatting | bytes 524288
